TPU v7x, 1024 devices: a whole 4x8x16 slice. The times are simulated.
1024 devices in a mesh: face: 128 (over z, y), tile: 8 (over x, core).
Axes of the slice: x: 4, y: 8, z: 16, core: 2. Of those that a mesh axis runs over, the one named last changes fastest.
Arguments:
- model_field: bfloat16 [2097152, 128], P(('face', 'tile')), may hold values from -6 to 6
- interp_weight: bfloat16 [262144, 2048], P(('face', 'tile')), may hold values from -0.125 to 0.125
- center_block: bfloat16 [262144, 256], P(('face', 'tile')), may hold values from -0.21875 to 0.21875
- lower_block: bfloat16 [262144, 256], P(('face', 'tile')), may hold values from -0.21875 to 0.21875
- upper_block: bfloat16 [262144, 256], P(('face', 'tile')), may hold values from -0.21875 to 0.21875
- owner_slots: int32 [1024, 256], P(('face', 'tile')), may hold values from 0 to 255, each once within a row
Outputs:
- localized: bfloat16 [2097152, 128], P(('face', 'tile'))
Inputs may be any that keep to these rules, and one draw needn't show every extreme that they name: `owner_slots`: each row is a permutation of 0 to 255.
All inputs are finite; a program needn't handle non-finite values.
Results may differ from a plain program's by a relative error of at most 0.013.
Values may be sent and summed in bfloat16 or wider, within the bound.
A program may use at most 32 MiB of HBM per device.

v0:
```python
import jax
import jax.numpy as jnp
from jax import lax
from jax.sharding import PartitionSpec as P


def extended(x, sides, width):
    for axis, dim in sides:
        size, length = (lax.axis_size(axis), x.shape[dim])
        up = [(i, (i + 1) % size) for i in range(size)]
        down = [(j, i) for i, j in up]
        last = lax.slice_in_dim(x, length - width, length, axis=dim)
        first = lax.slice_in_dim(x, 0, width, axis=dim)
        before = lax.ppermute(last, axis, up)
        after = lax.ppermute(first, axis, down)
        x = jnp.concatenate([before, x, after], axis=dim)
    return x


def from_behind(block, axis, distance):
    devices = range(lax.axis_size(axis))
    route = [((i - distance) % len(devices), i) for i in devices]
    return lax.ppermute(block, axis, route)


def left_product(block, field):
    return lax.dot_general(
        block, field, (((0,), (0,)), ((), ())), preferred_element_type=jnp.float32
    )


def local(model_field, interp_weight, center_block, lower_block, upper_block, owner_slots):
    points = center_block.shape[0]
    width = model_field.shape[1]
    subset = jnp.dot(interp_weight, model_field, preferred_element_type=jnp.float32).astype(
        jnp.bfloat16
    )
    slotted = jnp.take(subset, owner_slots[0], axis=0)
    owned = lax.all_to_all(slotted, "face", split_axis=0, concat_axis=0, tiled=True)
    padded = extended(owned, (("tile", 0),), points)
    below = padded[:points]
    above = padded[2 * points :]
    conv = jnp.dot(center_block, owned, preferred_element_type=jnp.float32)
    conv = conv + jnp.dot(lower_block, below, preferred_element_type=jnp.float32)
    conv = conv + jnp.dot(upper_block, above, preferred_element_type=jnp.float32)
    conv = conv.astype(jnp.bfloat16)
    own_term = left_product(center_block, conv)
    joined_low = jnp.concatenate([conv, lower_block], axis=1)
    joined_upp = jnp.concatenate([conv, upper_block], axis=1)
    from_next = from_behind(joined_low, "tile", -1)
    from_prev = from_behind(joined_upp, "tile", 1)
    low_term = left_product(from_next[:, width:], from_next[:, :width])
    upp_term = left_product(from_prev[:, width:], from_prev[:, :width])
    adjoint = (own_term + low_term + upp_term).astype(jnp.bfloat16)
    returned = lax.all_to_all(adjoint, "face", split_axis=0, concat_axis=0, tiled=True)
    back = jnp.zeros_like(returned).at[owner_slots[0]].set(returned)
    localized = left_product(interp_weight, back)
    return localized.astype(jnp.bfloat16)


def solution(mesh):
    placed = (
        P(("face", "tile"), None),
        P(("face", "tile"), None),
        P(("face", "tile"), None),
        P(("face", "tile"), None),
        P(("face", "tile"), None),
        P(("face", "tile"), None),
    )
    return jax.shard_map(
        local, mesh=mesh, in_specs=placed, out_specs=P(("face", "tile"), None), check_vma=False
    )
```

profile of v0, /device:TPU:8, one launch (start us, length us, event | category | flops | bytes accessed | tf_op | source)
XLA Modules:
  0.0 83.8 jit_solution(18405859020691049098)
XLA Ops:
  0.0 0.0 copy-start
  0.0 0.8 compare_select_fusion.1
  0.8 0.5 broadcast.38
  1.3 0.2 copy-done.4
  1.5 0.7 reduce.3
  2.1 0.1 squeeze.7
  2.3 1.5 %convolution_convert_fusion.1 = bf16[256,128]{1,0:T(8,128)(2,1)S(1)} fusion(bf16[256,2048]{1,0:T(8,128)(2,1)S(1)} %copy-done, bf16[2048,128]{1,0:T(8,128)(2,1)} %param.6), kind=kOutput, calls=%fused_computation.10 | convolution fusion | flops 134250496 | bytes 1638400 | tf_op jit(solution)/shard_map/dot_general | solution.py:35
  3.8 0.9 %gather_fusion = bf16[256,128]{1,0:T(8,128)(2,1)S(1)} fusion(bf16[256,128]{1,0:T(8,128)(2,1)S(1)} %convolution_convert_fusion.1, s32[1024]{0:T(1024)S(1)} %pad_clamp_fusion), kind=kCustom, calls=%fused_computation | custom fusion | bytes 132096 | tf_op jit(solution)/shard_map/jit(_take)/gather | solution.py:38
  4.6 0.2 broadcast_select_fusion
  4.9 41.5 %all_to_all.21 = bf16[128,2,128]{2,1,0:T(2,128)(2,1)S(1)} all-to-all(bf16[128,2,128]{2,1,0:T(2,128)(2,1)S(1)} %broadcast_select_fusion), channel_id=1, replica_groups=mesh['face'=128,'tile'=8] {'face'}, dimensions={0} | all-to-all | bytes 131072 | tf_op jit(solution)/shard_map/all_to_all | solution.py:39
  46.3 0.7 collective-permute-start.1
  47.0 0.0 collective-permute-start
  47.0 0.2 fusion.11
  47.2 0.0 copy-start.2
  47.2 4.7 %collective-permute-done = bf16[256,128]{1,0:T(8,128)(2,1)S(1)} collective-permute-done((bf16[256,128]{1,0:T(8,128)(2,1)S(1)}, bf16[256,128]{1,0:T(8,128)(2,1)S(1)}, u32[]{:S(2)}, u32[]{:S(2)}) %collective-permute-start) | collective-permute-done | bytes 65568 | tf_op jit(solution)/shard_map/ppermute | solution.py:14
  51.9 0.2 convolution_add_fusion.2
  52.1 0.0 collective-permute-done.1
  52.2 0.0 copy-done.2
  52.2 0.2 fusion.3
  52.4 0.1 copy.12
  52.6 0.0 collective-permute-start.2
  52.6 0.5 collective-permute-start.3
  53.1 0.2 convolution_bitcast_fusion
  53.2 5.7 %collective-permute-done.3 = bf16[256,384]{1,0:T(8,128)(2,1)S(1)} collective-permute-done((bf16[256,384]{1,0:T(8,128)(2,1)S(1)}, bf16[256,384]{1,0:T(8,128)(2,1)S(1)}, u32[]{:S(2)}, u32[]{:S(2)}) %collective-permute-start.3) | collective-permute-done | bytes 196640 | tf_op jit(solution)/shard_map/ppermute | solution.py:23
  58.9 0.2 fusion.4
  59.1 0.0 collective-permute-done.2
  59.1 0.2 fusion.2
  59.3 0.1 copy.16
  59.5 21.8 %all_to_all.22 = bf16[128,2,128]{2,1,0:T(2,128)(2,1)S(1)} all-to-all(bf16[128,2,128]{2,1,0:T(2,128)(2,1)S(1)} %bitcast.30), channel_id=1, replica_groups=mesh['face'=128,'tile'=8] {'face'}, dimensions={0} | all-to-all | bytes 131072 | tf_op jit(solution)/shard_map/all_to_all | solution.py:55
  81.2 1.2 %scatter_custom_fusion = bf16[256,128]{1,0:T(8,128)(2,1)S(1)} fusion(s32[256]{0:T(256)S(1)} %bitcast.33, bf16[256,128]{1,0:T(8,128)(2,1)S(1)} %bitcast.31, bf16[]{:T(256)} %constant.6.clone.1), kind=kCustom, calls=%fused_computation.22 | custom fusion | bytes 65538 | tf_op jit(solution)/shard_map/scatter | solution.py:56
  82.4 0.3 fusion
  82.8 1.0 %copy.17 = bf16[2048,128]{1,0:T(8,128)(2,1)} copy(bf16[2048,128]{0,1:T(8,128)(2,1)S(1)} %fusion) | data formatting | bytes 1048576 | tf_op jit(solution)/shard_map/convert_element_type | solution.py:58
  (9 shorter events, 0.1 us)
Async XLA Ops:
  0.0 2.3 %copy-start = (bf16[256,2048]{1,0:T(8,128)(2,1)S(1)}, bf16[256,2048]{1,0:T(8,128)(2,1)}, u32[]{:S(2)}) copy-start(bf16[256,2048]{1,0:T(8,128)(2,1)} %param.7) | copy-start | bytes 3145732
  0.8 0.7 copy-start.4
  4.6 42.4 %copy-start.3 = (bf16[256,256]{1,0:T(8,128)(2,1)S(1)}, bf16[256,256]{1,0:T(8,128)(2,1)}, u32[]{:S(2)}) copy-start(bf16[256,256]{1,0:T(8,128)(2,1)} %param.8) | copy-start | bytes 393220
  46.3 5.6 %copy-start.1 = (bf16[256,256]{1,0:T(8,128)(2,1)S(1)}, bf16[256,256]{1,0:T(8,128)(2,1)}, u32[]{:S(2)}) copy-start(bf16[256,256]{1,0:T(8,128)(2,1)} %param.9) | copy-start | bytes 393220
  46.3 5.8 %collective-permute-start.1 = (bf16[256,128]{1,0:T(8,128)(2,1)S(1)}, bf16[256,128]{1,0:T(8,128)(2,1)S(1)}, u32[]{:S(2)}, u32[]{:S(2)}) collective-permute-start(bf16[256,128]{1,0:T(8,128)(2,1)S(1)} %bitcast.26), channel_id=1, source_target_pairs={{1,0},{2,1},{3,2},{4,3},{5,4},{6,5},{7,6},{0,7},{9,8},{10,9},{11,1... | collective-permute-start | bytes 196616 | tf_op jit(solution)/shard_map/ppermute | solution.py:15
  47.0 4.9 %collective-permute-start = (bf16[256,128]{1,0:T(8,128)(2,1)S(1)}, bf16[256,128]{1,0:T(8,128)(2,1)S(1)}, u32[]{:S(2)}, u32[]{:S(2)}) collective-permute-start(bf16[256,128]{1,0:T(8,128)(2,1)S(1)} %bitcast.27), channel_id=1, source_target_pairs={{0,1},{1,2},{2,3},{3,4},{4,5},{5,6},{6,7},{7,0},{8,9},{9,10},{10,1... | collective-permute-start | bytes 196616 | tf_op jit(solution)/shard_map/ppermute | solution.py:14
  47.2 4.9 %copy-start.2 = (bf16[256,256]{1,0:T(8,128)(2,1)S(1)}, bf16[256,256]{1,0:T(8,128)(2,1)}, u32[]{:S(2)}) copy-start(bf16[256,256]{1,0:T(8,128)(2,1)} %param.10) | copy-start | bytes 393220
  52.6 6.6 %collective-permute-start.2 = (bf16[256,384]{1,0:T(8,128)(2,1)S(1)}, bf16[256,384]{1,0:T(8,128)(2,1)S(1)}, u32[]{:S(2)}, u32[]{:S(2)}) collective-permute-start(bf16[256,384]{1,0:T(8,128)(2,1)S(1)} %get-tuple-element.5), channel_id=1, source_target_pairs={{1,0},{2,1},{3,2},{4,3},{5,4},{6,5},{7,6},{0,7},{9,8},{10,9},{11,1... | collective-permute-start | bytes 589832 | tf_op jit(solution)/shard_map/ppermute | solution.py:23
  52.6 6.3 %collective-permute-start.3 = (bf16[256,384]{1,0:T(8,128)(2,1)S(1)}, bf16[256,384]{1,0:T(8,128)(2,1)S(1)}, u32[]{:S(2)}, u32[]{:S(2)}) collective-permute-start(bf16[256,384]{1,0:T(8,128)(2,1)S(1)} %get-tuple-element.6), channel_id=1, source_target_pairs={{7,0},{0,1},{1,2},{2,3},{3,4},{4,5},{5,6},{6,7},{15,8},{8,9},{9,10... | collective-permute-start | bytes 589832 | tf_op jit(solution)/shard_map/ppermute | solution.py:23
where the time goes:
time: 84 us; the launch traced here: 83.8 us
  blocking collectives  63.3 us (75%)
  waiting for transfers between devices  10.4 us (12%)
  local copies, waits for them, and re-layouts  4.1 us (5%)
  matrix products  2.98 us (4%)
  other arithmetic  1.72 us (2%)
  starting transfers between devices  1.22 us (1%)
    all_to_all x1, blocking collectives, local(): lax.all_to_all(slotted, 'face', split_axis=0, concat_axis=0, tiled=True)  41.5 us
    all_to_all x1, blocking collectives, local(): lax.all_to_all(adjoint, 'face', split_axis=0, concat_axis=0, tiled=True)  21.8 us
    ppermute x2, waiting for transfers between devices, from_behind(): return lax.ppermute(block, axis, route)  5.66 us
    ppermute x1, waiting for transfers between devices, extended(): before = lax.ppermute(last, axis, up)  4.69 us
  transfers between devices with their start and end apart: 4, of which 2 were waited for; matrix products, arithmetic and copies ran while one was open for 1% of the time, Pallas kernels for 0%

commit v1 on v0

v1 whole, which is shorter than its diff:
```python
import functools

import jax
import jax.numpy as jnp
from jax import lax
from jax.experimental import pallas as pl
from jax.experimental.pallas import tpu as pltpu
from jax.sharding import PartitionSpec as P

MESH = pl.DeviceIdType.MESH
F32, BF16 = jnp.float32, jnp.bfloat16
CHUNKS = 4


def dot(a, b, ca=1, cb=0):
    return lax.dot_general(a, b, (((ca,), (cb,)), ((), ())), preferred_element_type=F32)


def far_first(size):
    order = [size // 2] if size % 2 == 0 else []
    for d in range((size - 1) // 2, 0, -1):
        order += [d, size - d]
    return order


def kernel(
    ny, nz, nt,
    x_hbm, w_hbm, a_hbm, l_hbm, r_hbm, s_hbm, out_hbm,
    x_v, w_v, a_v, l_v, r_v, s_v, g_v, out_v,
    perm_v, swap_v, unswap_v,
    send1, recv1, send2, owned, below, above, low_out, upp_out, low_in, upp_in,
    send3, recv3, send4, recv4,
    load_sem, out_sem, send_sem, recv_sem,
):
    face, tile = lax.axis_index("face"), lax.axis_index("tile")
    z, y = lax.div(face, ny), lax.rem(face, ny)
    points, width = owned.shape
    share = points // (ny * nz)
    yrows, zrows = nz * share, ny * share
    depth = w_v.shape[1] // CHUNKS
    prev, nxt = lax.rem(tile + nt - 1, nt), lax.rem(tile + 1, nt)
    y_mates = [lax.rem(y + d, ny) for d in far_first(ny)]
    z_mates = [lax.rem(z + d, nz) for d in far_first(nz)]

    barrier = pltpu.get_barrier_semaphore()
    for m in z_mates:
        pl.semaphore_signal(barrier, inc=1, device_id={"face": m * ny + y}, device_id_type=MESH)
    for m in y_mates:
        pl.semaphore_signal(barrier, inc=1, device_id={"face": z * ny + m}, device_id_type=MESH)
    for m in (prev, nxt):
        pl.semaphore_signal(barrier, inc=1, device_id={"tile": m}, device_id_type=MESH)

    loads = [pltpu.make_async_copy(s_hbm, s_v, load_sem.at[0])]
    for c in range(CHUNKS):
        span = pl.ds(c * depth, depth)
        loads.append(pltpu.make_async_copy(x_hbm.at[span], x_v.at[span], load_sem.at[1 + 2 * c]))
        loads.append(pltpu.make_async_copy(w_hbm.at[:, span], w_v.at[:, span], load_sem.at[2 + 2 * c]))
    for i, (src, dst) in enumerate(((a_hbm, a_v), (l_hbm, l_v), (r_hbm, r_v))):
        loads.append(pltpu.make_async_copy(src, dst, load_sem.at[1 + 2 * CHUNKS + i]))
    for load in loads:
        load.start()

    rows = lax.broadcasted_iota(jnp.int32, (points, points), 0)
    cols = lax.broadcasted_iota(jnp.int32, (points, points), 1)

    def y_major(i):
        f, q = lax.div(i, share), lax.rem(i, share)
        return (lax.rem(f, ny) * nz + lax.div(f, ny)) * share + q

    swap_v[...] = jnp.where(cols == y_major(rows), 1.0, 0.0).astype(BF16)
    unswap_v[...] = jnp.where(rows == y_major(cols), 1.0, 0.0).astype(BF16)
    loads[0].wait()
    slots = jnp.broadcast_to(s_v[...].astype(F32), (points, points)).astype(BF16)
    slots = dot(unswap_v[...], slots, 1, 1)
    perm_v[...] = jnp.where(slots == cols.astype(F32), 1.0, 0.0).astype(BF16)

    total = None
    for c in range(CHUNKS):
        span = pl.ds(c * depth, depth)
        loads[1 + 2 * c].wait()
        loads[2 + 2 * c].wait()
        term = dot(w_v[:, span], x_v[span, :])
        total = term if total is None else total + term
    send1[...] = dot(perm_v[...], total.astype(BF16)).astype(BF16)

    pl.semaphore_wait(barrier, len(z_mates) + len(y_mates) + 2)

    def to_mates(phase, mates, face_of, mine, src, dst, size):
        here = pl.ds(pl.multiple_of(mine * size, size), size)
        copies = []
        for m in mates:
            copies.append(pltpu.make_async_remote_copy(
                src_ref=src.at[pl.ds(pl.multiple_of(m * size, size), size)],
                dst_ref=dst.at[here],
                send_sem=send_sem.at[phase],
                recv_sem=recv_sem.at[phase],
                device_id={"face": face_of(m)},
                device_id_type=MESH,
            ))
        for copy in copies:
            copy.start()
        dst[here, :] = src[here, :]
        span = pl.ds(0, size * len(mates))
        return pltpu.make_async_remote_copy(
            src_ref=src.at[span], dst_ref=dst.at[span],
            send_sem=send_sem.at[phase], recv_sem=recv_sem.at[phase],
            device_id={"face": face_of(mates[0])}, device_id_type=MESH,
        )

    def to_tile(phase, other, src, dst):
        copy = pltpu.make_async_remote_copy(
            src_ref=src, dst_ref=dst, send_sem=send_sem.at[phase], recv_sem=recv_sem.at[phase],
            device_id={"tile": other}, device_id_type=MESH,
        )
        copy.start()
        return copy

    waits = []
    waits.append(to_mates(0, y_mates, lambda m: z * ny + m, y, send1, recv1, yrows))
    for load in loads[1 + 2 * CHUNKS:]:
        load.wait()
    waits[-1].wait_recv()
    send2[...] = dot(swap_v[...], recv1[...]).astype(BF16)
    waits.append(to_mates(1, z_mates, lambda m: m * ny + y, z, send2, owned, zrows))
    for c in range(CHUNKS):
        span = pl.ds(c * depth, depth)
        g_v[span, :] = dot(w_v[:, span], perm_v[...], 0, 1).astype(BF16)
    waits[-1].wait_recv()

    waits.append(to_tile(2, nxt, owned, below))
    waits.append(to_tile(3, prev, owned, above))
    conv = dot(a_v[...], owned[...])
    waits[2].wait_recv()
    conv = conv + dot(l_v[...], below[...])
    waits[3].wait_recv()
    conv = (conv + dot(r_v[...], above[...])).astype(BF16)
    low_out[...] = dot(l_v[...], conv, 0, 0).astype(BF16)
    waits.append(to_tile(4, prev, low_out, low_in))
    upp_out[...] = dot(r_v[...], conv, 0, 0).astype(BF16)
    waits.append(to_tile(5, nxt, upp_out, upp_in))
    adjoint = dot(a_v[...], conv, 0, 0)
    waits[4].wait_recv()
    adjoint = adjoint + low_in[...].astype(F32)
    waits[5].wait_recv()
    send3[...] = (adjoint + upp_in[...].astype(F32)).astype(BF16)

    waits.append(to_mates(6, z_mates, lambda m: m * ny + y, z, send3, recv3, zrows))
    waits[-1].wait_recv()
    send4[...] = dot(unswap_v[...], recv3[...]).astype(BF16)
    waits.append(to_mates(7, y_mates, lambda m: z * ny + m, y, send4, recv4, yrows))
    waits[-1].wait_recv()

    stores = []
    for c in range(CHUNKS):
        span = pl.ds(c * depth, depth)
        out_v[span, :] = dot(g_v[span, :], recv4[...]).astype(BF16)
        stores.append(pltpu.make_async_copy(out_v.at[span], out_hbm.at[span], out_sem.at[c]))
        stores[-1].start()
    for wait in waits:
        wait.wait_send()
    for store in stores:
        store.wait()


def solution(mesh):
    nf, nt = mesh.shape["face"], mesh.shape["tile"]
    ny = 8 if nf == 128 else 2
    nz = nf // ny

    def local(model_field, interp_weight, center_block, lower_block, upper_block, owner_slots):
        model, width = model_field.shape
        points = interp_weight.shape[0]
        field = pltpu.VMEM((points, width), BF16)
        block = pltpu.VMEM((points, points), BF16)
        return pl.pallas_call(
            functools.partial(kernel, ny, nz, nt),
            out_shape=jax.ShapeDtypeStruct((model, width), BF16),
            in_specs=[pl.BlockSpec(memory_space=pl.ANY)] * 6,
            out_specs=pl.BlockSpec(memory_space=pl.ANY),
            scratch_shapes=[
                pltpu.VMEM((model, width), BF16),
                pltpu.VMEM((points, model), BF16),
                block, block, block,
                pltpu.VMEM((1, points), jnp.int32),
                pltpu.VMEM((model, points), BF16),
                pltpu.VMEM((model, width), BF16),
                block, block, block,
            ] + [field] * 14 + [
                pltpu.SemaphoreType.DMA((4 + 2 * CHUNKS,)),
                pltpu.SemaphoreType.DMA((CHUNKS,)),
                pltpu.SemaphoreType.DMA((8,)),
                pltpu.SemaphoreType.DMA((8,)),
            ],
            compiler_params=pltpu.CompilerParams(
                collective_id=0, has_side_effects=True, vmem_limit_bytes=24 * 2**20
            ),
            cost_estimate=pl.CostEstimate(
                flops=6 * points * model * width, bytes_accessed=6 * model * points, transcendentals=0
            ),
        )(model_field, interp_weight, center_block, lower_block, upper_block, owner_slots)

    placed = P(("face", "tile"), None)
    return jax.shard_map(
        local, mesh=mesh, in_specs=(placed,) * 6, out_specs=placed, check_vma=False
    )
```

time: 84 us -> 60.3 us (0.72)
  blocking collectives: 63.3 us -> 0 us
  Pallas kernels: 0 us -> 53.5 us
  waiting for transfers between devices: 10.4 us -> 0 us
  matrix products: 2.98 us -> 0 us
  local copies, waits for them, and re-layouts: 4.1 us -> 6.45 us
  other arithmetic: 1.72 us -> 0 us
  starting transfers between devices: 1.22 us -> 0 us
    all_to_all x2 -> x0, blocking collectives: 63.3 us -> none  [the longest x1 41.5 us: local(): lax.all_to_all(slotted, 'face', split_axis=0, concat_axis=0, tiled=True)]
    pallas_call x0 -> x1, Pallas kernels: none -> 53.5 us  [local(): pl.pallas_call(functools.partial(kernel, ny, nz, nt), out_shape=jax.Shape...]
    ppermute x4 -> x0, waiting for transfers between devices: 10.4 us -> none  [the longest x2 5.66 us: from_behind(): return lax.ppermute(block, axis, route)]
    unnamed x11 -> x13, local copies, waits for them, and re-layouts: 0.7 us -> 6.45 us
    dot_general x8 -> x0, matrix products: 2.98 us -> none  [the longest x1 1.47 us: local(): jnp.dot(interp_weight, model_field, preferred_element_type=jnp.float32)]
    convert_element_type x3 -> x0, local copies, waits for them, and re-layouts: 1.23 us -> none  [the longest x1 1 us: local(): return localized.astype(jnp.bfloat16)]
    ppermute x4 -> x0, starting transfers between devices: 1.22 us -> none  [the longest x1 0.71 us: extended(): after = lax.ppermute(first, axis, down)]
    scatter x1 -> x0, local copies, waits for them, and re-layouts: 1.18 us -> none  [local(): back = jnp.zeros_like(returned).at[owner_slots[0]].set(returned)]
  transfers between devices with their start and end apart: 4 -> 0, of which waited for: 2 -> 0; matrix products, arithmetic and copies ran while one was open for 1% -> 0% of each run, Pallas kernels for 0% -> 0%
where the time goes in v1:
time: 60.3 us; the launch traced here: 60 us
  Pallas kernels  53.5 us (89%)
  local copies, waits for them, and re-layouts  6.45 us (11%)
    pallas_call x1, Pallas kernels, local(): pl.pallas_call(functools.partial(kernel, ny, nz, nt), out_shape=jax.Shape...  53.5 us
    unnamed x13, local copies, waits for them, and re-layouts  6.45 us

profile of v1, /device:TPU:8, one launch (start us, length us, event | category | flops | bytes accessed | tf_op | source)
XLA Modules:
  0.0 60.0 jit_solution(3816887630571541033)
XLA Ops:
  0.0 0.0 copy-start
  0.0 1.2 %copy-done = bf16[256,2048]{1,0:T(8,128)(2,1)S(1)} copy-done((bf16[256,2048]{1,0:T(8,128)(2,1)S(1)}, bf16[256,2048]{1,0:T(8,128)(2,1)}, u32[]{:S(2)}) %copy-start) | copy-done | bytes 1048600
  1.2 0.0 copy-start.1
  1.2 1.0 %copy-done.1 = bf16[2048,128]{1,0:T(8,128)(2,1)S(1)} copy-done((bf16[2048,128]{1,0:T(8,128)(2,1)S(1)}, bf16[2048,128]{1,0:T(8,128)(2,1)}, u32[]{:S(2)}) %copy-start.1) | copy-done | bytes 524312
  2.3 0.0 copy-start.2
  2.3 0.9 %copy-done.2 = bf16[256,256]{1,0:T(8,128)(2,1)S(1)} copy-done((bf16[256,256]{1,0:T(8,128)(2,1)S(1)}, bf16[256,256]{1,0:T(8,128)(2,1)}, u32[]{:S(2)}) %copy-start.2) | copy-done | bytes 131096
  3.2 0.0 copy-start.3
  3.2 0.9 %copy-done.3 = bf16[256,256]{1,0:T(8,128)(2,1)S(1)} copy-done((bf16[256,256]{1,0:T(8,128)(2,1)S(1)}, bf16[256,256]{1,0:T(8,128)(2,1)}, u32[]{:S(2)}) %copy-start.3) | copy-done | bytes 131096
  4.1 0.0 copy-start.4
  4.1 0.9 %copy-done.4 = bf16[256,256]{1,0:T(8,128)(2,1)S(1)} copy-done((bf16[256,256]{1,0:T(8,128)(2,1)S(1)}, bf16[256,256]{1,0:T(8,128)(2,1)}, u32[]{:S(2)}) %copy-start.4) | copy-done | bytes 131096
  5.0 0.0 copy-start.5
  5.0 0.7 %copy-done.5 = s32[1,256]{1,0:T(1,128)S(1)} copy-done((s32[1,256]{1,0:T(1,128)S(1)}, s32[1,256]{1,0:T(1,128)}, u32[]{:S(2)}) %copy-start.5) | copy-done | bytes 1048
  5.7 53.5 %shard_map.64 = bf16[2048,128]{1,0:T(8,128)(2,1)S(1)} custom-call(bf16[2048,128]{1,0:T(8,128)(2,1)S(1)} %copy-done.1, bf16[256,2048]{1,0:T(8,128)(2,1)S(1)} %copy-done, bf16[256,256]{1,0:T(8,128)(2,1)S(1)} %copy-done.2, bf16[256,256]{1,0:T(8,128)(2,1)S(1)} %copy-done.3, bf16[256,256]{1,0:T(8,128)(2,1)S(1)} %copy-done.4, s32[1,256]{1,0:T(1,128)S(1)} %copy-done.5), custom_call_target="tpu_custom_call" | custom-call | flops 402653184 | bytes 3145728 | tf_op jit(solution)/shard_map/pallas_call | solution.py:175
  59.2 0.8 %copy.8 = bf16[2048,128]{1,0:T(8,128)(2,1)} copy(bf16[2048,128]{1,0:T(8,128)(2,1)S(1)} %shard_map.64) | data formatting | bytes 1048576
Async XLA Ops:
  0.0 1.2 %copy-start = (bf16[256,2048]{1,0:T(8,128)(2,1)S(1)}, bf16[256,2048]{1,0:T(8,128)(2,1)}, u32[]{:S(2)}) copy-start(bf16[256,2048]{1,0:T(8,128)(2,1)} %w_hbm.1) | copy-start | bytes 3145732
  1.2 1.0 %copy-start.1 = (bf16[2048,128]{1,0:T(8,128)(2,1)S(1)}, bf16[2048,128]{1,0:T(8,128)(2,1)}, u32[]{:S(2)}) copy-start(bf16[2048,128]{1,0:T(8,128)(2,1)} %x_hbm.1) | copy-start | bytes 1572868
  2.3 0.9 %copy-start.2 = (bf16[256,256]{1,0:T(8,128)(2,1)S(1)}, bf16[256,256]{1,0:T(8,128)(2,1)}, u32[]{:S(2)}) copy-start(bf16[256,256]{1,0:T(8,128)(2,1)} %a_hbm.1) | copy-start | bytes 393220
  3.2 0.9 %copy-start.3 = (bf16[256,256]{1,0:T(8,128)(2,1)S(1)}, bf16[256,256]{1,0:T(8,128)(2,1)}, u32[]{:S(2)}) copy-start(bf16[256,256]{1,0:T(8,128)(2,1)} %l_hbm.1) | copy-start | bytes 393220
  4.1 0.9 %copy-start.4 = (bf16[256,256]{1,0:T(8,128)(2,1)S(1)}, bf16[256,256]{1,0:T(8,128)(2,1)}, u32[]{:S(2)}) copy-start(bf16[256,256]{1,0:T(8,128)(2,1)} %r_hbm.1) | copy-start | bytes 393220
  5.0 0.7 %copy-start.5 = (s32[1,256]{1,0:T(1,128)S(1)}, s32[1,256]{1,0:T(1,128)}, u32[]{:S(2)}) copy-start(s32[1,256]{1,0:T(1,128)} %s_hbm.1) | copy-start | bytes 3076

commit v2 on v1

v2 whole, which is shorter than its diff:
```python
import functools

import jax
import jax.numpy as jnp
from jax import lax
from jax.experimental import pallas as pl
from jax.experimental.pallas import tpu as pltpu
from jax.sharding import PartitionSpec as P

MESH = pl.DeviceIdType.MESH
F32, BF16 = jnp.float32, jnp.bfloat16
CHUNKS = 4
OTHERS = (1, -1, 2, -2)


def dot(a, b, ca=1, cb=0):
    return lax.dot_general(a, b, (((ca,), (cb,)), ((), ())), preferred_element_type=F32)


def away(k, size):
    half = lax.div(k + 1, 2)
    return size // 2 + jnp.where(lax.rem(k, 2) == 1, -half, half)


def kernel(
    ny, nz, nt,
    x_hbm, w_hbm, a_hbm, l_hbm, r_hbm, s_hbm, back, w_v,
    x_v, s_v, perm_v, blocks, near, mixed,
    send1, owned3, owned, around, send2, recv2,
    load_sem, send_sem, recv_sem,
):
    face, tile = lax.axis_index("face"), lax.axis_index("tile")
    z, y = lax.div(face, ny), lax.rem(face, ny)
    faces, share, width = owned3.shape
    points = faces * share
    depth = w_v.shape[1] // CHUNKS

    def beside(d):
        return lax.rem(tile + nt + d, nt)

    def to_each_mate(act):
        def step(i, carry):
            dz, dy = away(lax.div(i, ny), nz), away(lax.rem(i, ny), ny)
            act(lax.rem(z + dz, nz) * ny + lax.rem(y + dy, ny))
            return carry

        lax.fori_loop(0, faces - 1, step, 0)

    barrier = pltpu.get_barrier_semaphore()
    to_each_mate(lambda m: pl.semaphore_signal(barrier, inc=1, device_id={"face": m}, device_id_type=MESH))
    for d in OTHERS:
        pl.semaphore_signal(barrier, inc=1, device_id={"tile": beside(d)}, device_id_type=MESH)

    def load(c):
        span = pl.ds(pl.multiple_of(c * depth, depth), depth)
        return (
            pltpu.make_async_copy(x_hbm.at[span], x_v.at[span], load_sem.at[2 * c]),
            pltpu.make_async_copy(w_hbm.at[:, span], w_v.at[:, span], load_sem.at[2 * c + 1]),
        )

    for c in range(CHUNKS):
        for copy in load(c):
            copy.start()
    loads = []
    for i, (src, dst) in enumerate(((s_hbm, s_v), (a_hbm, blocks.at[0]), (l_hbm, blocks.at[1]), (r_hbm, blocks.at[2]))):
        loads.append(pltpu.make_async_copy(src, dst, load_sem.at[2 * CHUNKS + i]))
        loads[-1].start()

    def add(c, total):
        span = pl.ds(pl.multiple_of(c * depth, depth), depth)
        for copy in load(c):
            copy.wait()
        return total + dot(w_v[:, span], x_v[span, :])

    total = lax.fori_loop(0, CHUNKS, add, jnp.zeros((points, width), F32))
    loads[0].wait()
    rows = lax.broadcasted_iota(jnp.int32, (points, points), 0)
    perm_v[...] = jnp.where(rows == s_v[...], 1.0, 0.0).astype(BF16)
    send1[...] = dot(perm_v[...], total.astype(BF16), 0, 0).astype(BF16).reshape(faces, share, width)
    for copy in loads[1:]:
        copy.wait()

    pl.semaphore_wait(barrier, faces - 1 + len(OTHERS))

    def to_mates(phase, src, dst):
        to_each_mate(lambda m: pltpu.make_async_remote_copy(
            src_ref=src.at[m], dst_ref=dst.at[face],
            send_sem=send_sem.at[phase], recv_sem=recv_sem.at[phase],
            device_id={"face": m}, device_id_type=MESH,
        ).start())
        dst[face] = src[face]
        span = pl.ds(0, faces - 1)
        return pltpu.make_async_remote_copy(
            src_ref=src.at[span], dst_ref=dst.at[span],
            send_sem=send_sem.at[phase], recv_sem=recv_sem.at[phase],
            device_id={"face": lax.rem(face + 1, faces)}, device_id_type=MESH,
        )

    def to_tile(phase, other, src, dst):
        copy = pltpu.make_async_remote_copy(
            src_ref=src, dst_ref=dst, send_sem=send_sem.at[phase], recv_sem=recv_sem.at[phase],
            device_id={"tile": other}, device_id_type=MESH,
        )
        copy.start()
        return copy

    waits = []
    waits.append(to_mates(0, send1, owned3))
    waits.append(to_tile(1, beside(-1), blocks, near.at[1]))
    waits.append(to_tile(2, beside(1), blocks, near.at[0]))
    waits[0].wait_recv()
    owned[...] = owned3[...].reshape(points, width)

    fields = [to_tile(3 + k, beside(-OTHERS[k]), owned, around.at[k]) for k in (2, 3, 0, 1)]
    waits += fields
    waits[1].wait_recv()
    waits[2].wait_recv()

    a, l, r = (blocks[i] for i in range(3))
    ap, lp, rp = (near[0, i] for i in range(3))
    an, ln, rn = (near[1, i] for i in range(3))
    mixed[0] = (dot(a, a, 0, 0) + dot(ln, ln, 0, 0) + dot(rp, rp, 0, 0)).astype(BF16)
    mixed[1] = (dot(a, r, 0, 0) + dot(ln, an, 0, 0)).astype(BF16)
    mixed[2] = (dot(a, l, 0, 0) + dot(rp, ap, 0, 0)).astype(BF16)
    mixed[3] = dot(ln, rn, 0, 0).astype(BF16)
    mixed[4] = dot(rp, lp, 0, 0).astype(BF16)
    adjoint = dot(mixed[0], owned[...])
    for k, field in ((0, fields[2]), (1, fields[3]), (2, fields[0]), (3, fields[1])):
        field.wait_recv()
        adjoint = adjoint + dot(mixed[1 + k], around[k])
    send2[...] = adjoint.astype(BF16).reshape(faces, share, width)

    waits.append(to_mates(7, send2, recv2))
    waits[-1].wait_recv()
    back[...] = dot(perm_v[...], recv2[...].reshape(points, width)).astype(BF16)
    for wait in waits:
        wait.wait_send()


def spread(w_ref, back_ref, out_hbm, out_v, out_sem):
    depth = w_ref.shape[1] // CHUNKS

    stores = []
    for c in range(CHUNKS):
        span = pl.ds(c * depth, depth)
        out_v[span, :] = dot(w_ref[:, span], back_ref[...], 0, 0).astype(BF16)
        stores.append(pltpu.make_async_copy(out_v.at[span], out_hbm.at[span], out_sem.at[c]))
        stores[-1].start()
    for store in stores:
        store.wait()


def solution(mesh):
    nf, nt = mesh.shape["face"], mesh.shape["tile"]
    ny = 8 if nf == 128 else 2
    nz = nf // ny

    def local(model_field, interp_weight, center_block, lower_block, upper_block, owner_slots):
        model, width = model_field.shape
        points = interp_weight.shape[0]
        field = pltpu.VMEM((points, width), BF16)
        field3 = pltpu.VMEM((nf, points // nf, width), BF16)
        back, weight = pl.pallas_call(
            functools.partial(kernel, ny, nz, nt),
            out_shape=(
                jax.ShapeDtypeStruct((points, width), BF16),
                jax.ShapeDtypeStruct((points, model), BF16),
            ),
            in_specs=[pl.BlockSpec(memory_space=pltpu.HBM)] * 6,
            out_specs=[pl.BlockSpec(memory_space=pltpu.VMEM)] * 2,
            scratch_shapes=[
                pltpu.VMEM((model, width), BF16),
                pltpu.VMEM((1, points), jnp.int32),
                pltpu.VMEM((points, points), BF16),
                pltpu.VMEM((3, points, points), BF16),
                pltpu.VMEM((2, 3, points, points), BF16),
                pltpu.VMEM((5, points, points), BF16),
                field3, field3, field, pltpu.VMEM((4, points, width), BF16), field3, field3,
                pltpu.SemaphoreType.DMA((4 + 2 * CHUNKS,)),
                pltpu.SemaphoreType.DMA((8,)),
                pltpu.SemaphoreType.DMA((8,)),
            ],
            compiler_params=pltpu.CompilerParams(
                collective_id=0, has_side_effects=True, vmem_limit_bytes=16 * 2**20
            ),
            cost_estimate=pl.CostEstimate(
                flops=6 * points * model * width, bytes_accessed=6 * model * points, transcendentals=0
            ),
        )(*(pltpu.with_memory_space_constraint(v, pltpu.HBM) for v in (
            model_field, interp_weight, center_block, lower_block, upper_block, owner_slots
        )))
        return pl.pallas_call(
            spread,
            out_shape=jax.ShapeDtypeStruct((model, width), BF16),
            in_specs=[pl.BlockSpec(memory_space=pltpu.VMEM)] * 2,
            out_specs=pl.BlockSpec(memory_space=pltpu.HBM),
            scratch_shapes=[pltpu.VMEM((model, width), BF16), pltpu.SemaphoreType.DMA((CHUNKS,))],
            compiler_params=pltpu.CompilerParams(vmem_limit_bytes=16 * 2**20),
            cost_estimate=pl.CostEstimate(
                flops=2 * points * model * width, bytes_accessed=4 * model * points, transcendentals=0
            ),
        )(weight, back)

    placed = P(("face", "tile"), None)
    return jax.shard_map(
        local, mesh=mesh, in_specs=(placed,) * 6, out_specs=placed, check_vma=False
    )
```

time: 60.3 us -> 51.4 us (0.85)
  the two profiles are of different devices: /device:TPU:8 before, /device:TPU:1 now
where the time goes in v2:
time: 51.4 us; the launch traced here: 51.3 us
  Pallas kernels  51.3 us (100%)
    pallas_call x1, Pallas kernels, local(): pl.pallas_call(functools.partial(kernel, ny, nz, nt), out_shape=(jax.Shap...  50.1 us
    pallas_call x1, Pallas kernels, local(): pl.pallas_call(spread, out_shape=jax.ShapeDtypeStruct((model, width), BF1...  1.19 us

profile of v2, /device:TPU:1, one launch (start us, length us, event | category | flops | bytes accessed | tf_op | source)
XLA Modules:
  0.0 51.3 jit_solution(13146797543053397242)
XLA Ops:
  0.0 50.1 %shard_map.64 = (bf16[256,128]{1,0:T(8,128)(2,1)S(1)}, bf16[256,2048]{1,0:T(8,128)(2,1)S(1)}) custom-call(bf16[2048,128]{1,0:T(8,128)(2,1)} %x_hbm.1, bf16[256,2048]{1,0:T(8,128)(2,1)} %w_hbm.1, bf16[256,256]{1,0:T(8,128)(2,1)} %a_hbm.1, bf16[256,256]{1,0:T(8,128)(2,1)} %l_hbm.1, bf16[256,256]{1,0:T(8,128)(2,1)} %r_hbm.1, s32[1,256]{1,0:T(1,128)} %s_hbm.1), custom_call_target="tpu_custom_call" | custom-call | flops 402653184 | bytes 3145728 | tf_op jit(solution)/shard_map/pallas_call | solution.py:163
  50.1 1.2 %shard_map.65 = bf16[2048,128]{1,0:T(8,128)(2,1)} custom-call(bf16[256,2048]{1,0:T(8,128)(2,1)S(1)} %get-tuple-element.7.w_ref, bf16[256,128]{1,0:T(8,128)(2,1)S(1)} %get-tuple-element.8.back_ref), custom_call_target="tpu_custom_call" | custom-call | flops 134217728 | bytes 2097152 | tf_op jit(solution)/shard_map/pallas_call | solution.py:192

commit v3 on v2

v3 whole, which is shorter than its diff:
```python
import functools

import jax
import jax.numpy as jnp
from jax import lax
from jax.experimental import pallas as pl
from jax.experimental.pallas import tpu as pltpu
from jax.sharding import PartitionSpec as P

MESH = pl.DeviceIdType.MESH
F32, BF16 = jnp.float32, jnp.bfloat16
LOADS = 2
STORES = 4
OTHERS = (1, -1, 2, -2)


def dot(a, b, ca=1, cb=0):
    return lax.dot_general(a, b, (((ca,), (cb,)), ((), ())), preferred_element_type=F32)


def away(k, size):
    half = lax.div(k + 1, 2)
    return size // 2 + jnp.where(lax.rem(k, 2) == 1, -half, half)


def kernel(
    ny, nz, nt,
    x_hbm, w_hbm, a_hbm, l_hbm, r_hbm, s_hbm, returned, weight,
    x_v, w_v, s_v, perm_v, blocks, near, mixed,
    send1, owned, around, send2, recv2,
    load_sem, send_sem, recv_sem,
):
    face, tile = lax.axis_index("face"), lax.axis_index("tile")
    z, y = lax.div(face, ny), lax.rem(face, ny)
    faces, share, width = owned.shape
    points = faces * share
    depth = w_v.shape[1] // LOADS
    far = max(1, nz * 7 // 16)

    def beside(d):
        return lax.rem(tile + nt + d, nt)

    def plane(k):
        return lax.rem(z + away(k, nz), nz)

    def to_mates(act, first=0, last=faces - 1):
        def step(i, carry):
            act(plane(lax.div(i, ny)) * ny + lax.rem(y + away(lax.rem(i, ny), ny), ny))
            return carry

        lax.fori_loop(first, last, step, 0)

    loads = []
    for c in range(LOADS):
        span = pl.ds(c * depth, depth)
        loads.append(pltpu.make_async_copy(x_hbm.at[span], x_v.at[span], load_sem.at[2 * c]))
        loads.append(pltpu.make_async_copy(w_hbm.at[:, span], w_v.at[:, span], load_sem.at[2 * c + 1]))
    for copy in loads:
        copy.start()

    barrier = pltpu.get_barrier_semaphore()
    to_mates(lambda m: pl.semaphore_signal(barrier, inc=1, device_id={"face": m}, device_id_type=MESH))
    for d in OTHERS:
        pl.semaphore_signal(barrier, inc=1, device_id={"tile": beside(d)}, device_id_type=MESH)

    for i, (src, dst) in enumerate((
        (s_hbm, s_v), (a_hbm, blocks.at[0]), (l_hbm, blocks.at[1]), (r_hbm, blocks.at[2])
    )):
        loads.append(pltpu.make_async_copy(src, dst, load_sem.at[2 * LOADS + i]))
        loads[-1].start()

    total = None
    for c in range(LOADS):
        span = pl.ds(c * depth, depth)
        loads[2 * c].wait()
        loads[2 * c + 1].wait()
        term = dot(w_v[:, span], x_v[span, :])
        total = term if total is None else total + term
    loads[2 * LOADS].wait()
    rows = lax.broadcasted_iota(jnp.int32, (points, points), 0)
    perm_v[...] = jnp.where(rows == s_v[...], 1.0, 0.0).astype(BF16)
    send1[...] = dot(perm_v[...], total.astype(BF16), 0, 0).astype(BF16).reshape(faces, share, width)
    owned[face] = send1[face]
    for copy in loads[2 * LOADS + 1:]:
        copy.wait()

    pl.semaphore_wait(barrier, faces - 1 + len(OTHERS))

    def remote(src, dst, phase, other):
        return pltpu.make_async_remote_copy(
            src_ref=src, dst_ref=dst, send_sem=send_sem.at[phase], recv_sem=recv_sem.at[phase],
            device_id=other, device_id_type=MESH,
        )

    def exchange(phase, src, dst, first, last):
        to_mates(lambda m: remote(src.at[m], dst.at[face], phase, {"face": m}).start(), first, last)
        span = pl.ds(0, last - first)
        return remote(src.at[span], dst.at[span], phase, {"face": lax.rem(face + 1, faces)})

    far_half = exchange(0, send1, owned, 0, far * ny)
    near_half = exchange(1, send1, owned, far * ny, faces - 1)
    to_prev = remote(blocks, near.at[1], 2, {"tile": beside(-1)})
    to_next = remote(blocks, near.at[0], 3, {"tile": beside(1)})
    to_prev.start()
    to_next.start()
    waits = [far_half, near_half, to_prev, to_next]
    weight[...] = dot(w_v[...], perm_v[...], 0, 0).astype(BF16)

    def hand_on(first, last):
        def step(k, carry):
            span = pl.ds(plane(k) * ny, ny)
            for j in (2, 3, 0, 1):
                remote(owned.at[span], around.at[j, span], 4 + j, {"tile": beside(-OTHERS[j])}).start()
            return carry

        lax.fori_loop(first, last, step, 0)

    near_half.wait_recv()
    hand_on(far, nz)
    far_half.wait_recv()
    hand_on(0, far)
    fields = [remote(owned, around.at[j], 4 + j, {"tile": beside(-d)}) for j, d in enumerate(OTHERS)]
    waits += fields

    to_prev.wait_recv()
    to_next.wait_recv()
    a, l, r = (blocks[i] for i in range(3))
    ap, lp, rp = (near[0, i] for i in range(3))
    an, ln, rn = (near[1, i] for i in range(3))
    mixed[0] = (dot(a, a, 0, 0) + dot(ln, ln, 0, 0) + dot(rp, rp, 0, 0)).astype(BF16)
    mixed[1] = (dot(a, r, 0, 0) + dot(ln, an, 0, 0)).astype(BF16)
    mixed[2] = (dot(a, l, 0, 0) + dot(rp, ap, 0, 0)).astype(BF16)
    mixed[3] = dot(ln, rn, 0, 0).astype(BF16)
    mixed[4] = dot(rp, lp, 0, 0).astype(BF16)
    adjoint = dot(mixed[0], owned[...].reshape(points, width))
    for j, field in enumerate(fields):
        field.wait_recv()
        adjoint = adjoint + dot(mixed[1 + j], around[j].reshape(points, width))
    send2[...] = adjoint.astype(BF16).reshape(faces, share, width)

    waits.append(exchange(8, send2, recv2, 0, faces - 1))
    recv2[face] = send2[face]
    waits[-1].wait_recv()
    returned[...] = recv2[...].reshape(points, width)
    for wait in waits:
        wait.wait_send()


def spread(weight_ref, returned_ref, out_hbm, out_v, out_sem):
    depth = weight_ref.shape[0] // STORES
    stores = []
    for c in range(STORES):
        span = pl.ds(c * depth, depth)
        out_v[span, :] = dot(weight_ref[span, :], returned_ref[...]).astype(BF16)
        stores.append(pltpu.make_async_copy(out_v.at[span], out_hbm.at[span], out_sem.at[c]))
        stores[-1].start()
    for store in stores:
        store.wait()


def solution(mesh):
    nf, nt = mesh.shape["face"], mesh.shape["tile"]
    ny = 8 if nf == 128 else 2
    nz = nf // ny

    def local(model_field, interp_weight, center_block, lower_block, upper_block, owner_slots):
        model, width = model_field.shape
        points = interp_weight.shape[0]
        field = pltpu.VMEM((nf, points // nf, width), BF16)
        returned, weight = pl.pallas_call(
            functools.partial(kernel, ny, nz, nt),
            out_shape=(
                jax.ShapeDtypeStruct((points, width), BF16),
                jax.ShapeDtypeStruct((model, points), BF16),
            ),
            in_specs=[pl.BlockSpec(memory_space=pltpu.HBM)] * 6,
            out_specs=[pl.BlockSpec(memory_space=pltpu.VMEM)] * 2,
            scratch_shapes=[
                pltpu.VMEM((model, width), BF16),
                pltpu.VMEM((points, model), BF16),
                pltpu.VMEM((1, points), jnp.int32),
                pltpu.VMEM((points, points), BF16),
                pltpu.VMEM((3, points, points), BF16),
                pltpu.VMEM((2, 3, points, points), BF16),
                pltpu.VMEM((5, points, points), BF16),
                field, field, pltpu.VMEM((4, nf, points // nf, width), BF16), field, field,
                pltpu.SemaphoreType.DMA((4 + 2 * LOADS,)),
                pltpu.SemaphoreType.DMA((9,)),
                pltpu.SemaphoreType.DMA((9,)),
            ],
            compiler_params=pltpu.CompilerParams(
                collective_id=0, has_side_effects=True, vmem_limit_bytes=16 * 2**20
            ),
            cost_estimate=pl.CostEstimate(
                flops=6 * points * model * width, bytes_accessed=6 * model * points, transcendentals=0
            ),
        )(*(pltpu.with_memory_space_constraint(v, pltpu.HBM) for v in (
            model_field, interp_weight, center_block, lower_block, upper_block, owner_slots
        )))
        return pl.pallas_call(
            spread,
            out_shape=jax.ShapeDtypeStruct((model, width), BF16),
            in_specs=[pl.BlockSpec(memory_space=pltpu.VMEM)] * 2,
            out_specs=pl.BlockSpec(memory_space=pltpu.HBM),
            scratch_shapes=[pltpu.VMEM((model, width), BF16), pltpu.SemaphoreType.DMA((STORES,))],
            compiler_params=pltpu.CompilerParams(vmem_limit_bytes=16 * 2**20),
            cost_estimate=pl.CostEstimate(
                flops=2 * points * model * width, bytes_accessed=4 * model * points, transcendentals=0
            ),
        )(weight, returned)

    placed = P(("face", "tile"), None)
    return jax.shard_map(
        local, mesh=mesh, in_specs=(placed,) * 6, out_specs=placed, check_vma=False
    )
```

time: 51.4 us -> 50.8 us (0.988)
  Pallas kernels: 51.3 us -> 50.6 us
    pallas_call x1, Pallas kernels: 50.1 us -> 49.5 us  [local(): pl.pallas_call(functools.partial(kernel, ny, nz, nt), out_shape=(jax.Shap...]
where the time goes in v3:
time: 50.8 us; the launch traced here: 50.6 us
  Pallas kernels  50.6 us (100%)
    pallas_call x1, Pallas kernels, local(): pl.pallas_call(functools.partial(kernel, ny, nz, nt), out_shape=(jax.Shap...  49.5 us
    pallas_call x1, Pallas kernels, local(): pl.pallas_call(spread, out_shape=jax.ShapeDtypeStruct((model, width), BF1...  1.17 us

profile of v3, /device:TPU:1, one launch (start us, length us, event | category | flops | bytes accessed | tf_op | source)
XLA Modules:
  0.0 50.6 jit_solution(2195559908166219969)
XLA Ops:
  0.0 49.5 %shard_map.64 = (bf16[256,128]{1,0:T(8,128)(2,1)S(1)}, bf16[2048,256]{1,0:T(8,128)(2,1)S(1)}) custom-call(bf16[2048,128]{1,0:T(8,128)(2,1)} %x_hbm.1, bf16[256,2048]{1,0:T(8,128)(2,1)} %w_hbm.1, bf16[256,256]{1,0:T(8,128)(2,1)} %a_hbm.1, bf16[256,256]{1,0:T(8,128)(2,1)} %l_hbm.1, bf16[256,256]{1,0:T(8,128)(2,1)} %r_hbm.1, s32[1,256]{1,0:T(1,128)} %s_hbm.1), custom_call_target="tpu_custom_call" | custom-call | flops 402653184 | bytes 3145728 | tf_op jit(solution)/shard_map/pallas_call | solution.py:170
  49.5 1.2 %shard_map.65 = bf16[2048,128]{1,0:T(8,128)(2,1)} custom-call(bf16[2048,256]{1,0:T(8,128)(2,1)S(1)} %get-tuple-element.7.weight_ref, bf16[256,128]{1,0:T(8,128)(2,1)S(1)} %get-tuple-element.8.returned_ref), custom_call_target="tpu_custom_call" | custom-call | flops 134217728 | bytes 2097152 | tf_op jit(solution)/shard_map/pallas_call | solution.py:200

commit v4 on v3

--- a/solution.py
+++ b/solution.py
@@ -35,7 +35,8 @@
     faces, share, width = owned.shape
     points = faces * share
     depth = w_v.shape[1] // LOADS
-    far = max(1, nz * 7 // 16)
+    cuts = sorted({0, max(1, nz * 3 // 16), max(1, nz * 5 // 16), max(1, nz * 9 // 16), nz})
+    groups = list(zip(cuts[:-1], cuts[1:]))
 
     def beside(d):
         return lax.rem(tile + nt + d, nt)
@@ -97,13 +98,15 @@
         span = pl.ds(0, last - first)
         return remote(src.at[span], dst.at[span], phase, {"face": lax.rem(face + 1, faces)})
 
-    far_half = exchange(0, send1, owned, 0, far * ny)
-    near_half = exchange(1, send1, owned, far * ny, faces - 1)
+    parts = [
+        exchange(9 + i, send1, owned, first * ny, min(last * ny, faces - 1))
+        for i, (first, last) in enumerate(groups)
+    ]
     to_prev = remote(blocks, near.at[1], 2, {"tile": beside(-1)})
     to_next = remote(blocks, near.at[0], 3, {"tile": beside(1)})
     to_prev.start()
     to_next.start()
-    waits = [far_half, near_half, to_prev, to_next]
+    waits = parts + [to_prev, to_next]
     weight[...] = dot(w_v[...], perm_v[...], 0, 0).astype(BF16)
 
     def hand_on(first, last):
@@ -115,10 +118,9 @@
 
         lax.fori_loop(first, last, step, 0)
 
-    near_half.wait_recv()
-    hand_on(far, nz)
-    far_half.wait_recv()
-    hand_on(0, far)
+    for part, (first, last) in reversed(list(zip(parts, groups))):
+        part.wait_recv()
+        hand_on(first, last)
     fields = [remote(owned, around.at[j], 4 + j, {"tile": beside(-d)}) for j, d in enumerate(OTHERS)]
     waits += fields
 
@@ -185,8 +187,8 @@
                 pltpu.VMEM((5, points, points), BF16),
                 field, field, pltpu.VMEM((4, nf, points // nf, width), BF16), field, field,
                 pltpu.SemaphoreType.DMA((4 + 2 * LOADS,)),
-                pltpu.SemaphoreType.DMA((9,)),
-                pltpu.SemaphoreType.DMA((9,)),
+                pltpu.SemaphoreType.DMA((13,)),
+                pltpu.SemaphoreType.DMA((13,)),
             ],
             compiler_params=pltpu.CompilerParams(
                 collective_id=0, has_side_effects=True, vmem_limit_bytes=16 * 2**20

time: 50.8 us -> 50.5 us (level)
  no operation moved by 1% of the time
where the time goes in v4:
time: 50.5 us; the launch traced here: 50.4 us
  Pallas kernels  50.4 us (100%)
    pallas_call x1, Pallas kernels, local(): pl.pallas_call(functools.partial(kernel, ny, nz, nt), out_shape=(jax.Shap...  49.2 us
    pallas_call x1, Pallas kernels, local(): pl.pallas_call(spread, out_shape=jax.ShapeDtypeStruct((model, width), BF1...  1.17 us

profile of v4, /device:TPU:1, one launch (start us, length us, event | category | flops | bytes accessed | tf_op | source)
XLA Modules:
  0.0 50.4 jit_solution(7504273427050776707)
XLA Ops:
  0.0 49.2 %shard_map.64 = (bf16[256,128]{1,0:T(8,128)(2,1)S(1)}, bf16[2048,256]{1,0:T(8,128)(2,1)S(1)}) custom-call(bf16[2048,128]{1,0:T(8,128)(2,1)} %x_hbm.1, bf16[256,2048]{1,0:T(8,128)(2,1)} %w_hbm.1, bf16[256,256]{1,0:T(8,128)(2,1)} %a_hbm.1, bf16[256,256]{1,0:T(8,128)(2,1)} %l_hbm.1, bf16[256,256]{1,0:T(8,128)(2,1)} %r_hbm.1, s32[1,256]{1,0:T(1,128)} %s_hbm.1), custom_call_target="tpu_custom_call" | custom-call | flops 402653184 | bytes 3145728 | tf_op jit(solution)/shard_map/pallas_call | solution.py:172
  49.2 1.2 %shard_map.65 = bf16[2048,128]{1,0:T(8,128)(2,1)} custom-call(bf16[2048,256]{1,0:T(8,128)(2,1)S(1)} %get-tuple-element.7.weight_ref, bf16[256,128]{1,0:T(8,128)(2,1)S(1)} %get-tuple-element.8.returned_ref), custom_call_target="tpu_custom_call" | custom-call | flops 134217728 | bytes 2097152 | tf_op jit(solution)/shard_map/pallas_call | solution.py:202
